TPU v7x, 32 devices: a whole 2x2x4 slice. The times are simulated.
32 devices in a mesh: grp: 2 (over y), wt: 4 (over x, core), tm: 4 (over z).
Axes of the slice: x: 2, y: 2, z: 4, core: 2. Of those that a mesh axis runs over, the one named last changes fastest.
Arguments:
- signal: bfloat16 [5120, 512], P(('grp', 'tm')), parts along dimension 0, may hold values from -6 to 6
- cotangent: bfloat16 [5120, 512], P(('grp', 'tm')), parts along dimension 0, may hold values from -6 to 6
- first_filter_taps: bfloat16 [3, 512, 1024], P(None, None, 'wt'), may hold values from -0.15625 to 0.15625
- first_gate_taps: bfloat16 [3, 512, 1024], P(None, None, 'wt'), may hold values from -0.15625 to 0.15625
- first_residual_projection: bfloat16 [1024, 512], P('wt'), may hold values from -0.1875 to 0.1875
- second_filter_taps: bfloat16 [3, 512, 1024], P(None, None, 'wt'), may hold values from -0.15625 to 0.15625
- second_gate_taps: bfloat16 [3, 512, 1024], P(None, None, 'wt'), may hold values from -0.15625 to 0.15625
- second_residual_projection: bfloat16 [1024, 512], P('wt'), may hold values from -0.1875 to 0.1875
Outputs:
- second_layer_output: bfloat16 [5120, 512], P(('grp', 'tm', 'wt')), parts along dimension 0
- input_feature_gradient: bfloat16 [5120, 512], P(('grp', 'tm')), parts along dimension 0
- grad_filter_first: float32 [6, 512, 1024], P('grp', 'tm', 'wt'), parts along dimension 0
- grad_gate_first: float32 [6, 512, 1024], P('grp', 'tm', 'wt'), parts along dimension 0
- grad_mix_first: float32 [2048, 512], P(('grp', 'wt'), 'tm'), parts along dimension 0
- grad_filter_second: float32 [6, 512, 1024], P('grp', 'tm', 'wt'), parts along dimension 0
- grad_gate_second: float32 [6, 512, 1024], P('grp', 'tm', 'wt'), parts along dimension 0
- grad_mix_second: float32 [2048, 512], P(('grp', 'wt'), 'tm'), parts along dimension 0
There are 2 independent parts, one for each index of `grp`. A program takes and returns all parts, laid end to end along the dimension named above; an argument that names none is the same for every part. Nothing has to cross between parts.
All inputs are finite; a program needn't handle non-finite values.
Results may differ from a plain program's by a relative error of at most 0.0065.
Values may be sent and summed in bfloat16 or wider, within the bound.
A program may use at most 64 MiB of HBM per device.

v0:
```python
import math

import jax
import jax.numpy as jnp
from jax import lax
from jax.sharding import PartitionSpec as P


def shifted(block, axis, distance):
    devices = range(lax.axis_size(axis))
    route = [(i - distance, i) for i in devices if i - distance in devices]
    return lax.ppermute(block, axis, route)


def contract_rows(left_side, right_side):
    return lax.dot_general(
        left_side, right_side, (((0,), (0,)), ((), ())), preferred_element_type=jnp.float32
    )


def contract_cols(left_side, right_side):
    return lax.dot_general(
        left_side, right_side, (((1,), (1,)), ((), ())), preferred_element_type=jnp.float32
    )


def apply_taps(tap_inputs, stacked):
    preact = jnp.dot(tap_inputs[0], stacked[0], preferred_element_type=jnp.float32)
    preact = preact + jnp.dot(tap_inputs[1], stacked[1], preferred_element_type=jnp.float32)
    return preact + jnp.dot(tap_inputs[2], stacked[2], preferred_element_type=jnp.float32)


def preact_short(signal, stacked):
    seg_rows = signal.shape[0]
    midpoint = seg_rows // 2
    earlier = shifted(signal, "tm", 1)
    joined = jnp.concatenate([earlier, signal], axis=0)
    tap_inputs = (signal, joined[midpoint : midpoint + seg_rows], earlier)
    return (apply_taps(tap_inputs, stacked), tap_inputs)


def preact_long(signal, stacked):
    one_back = shifted(signal, "tm", 1)
    two_back = shifted(signal, "tm", 2)
    tap_inputs = (signal, one_back, two_back)
    return (apply_taps(tap_inputs, stacked), tap_inputs)


def gate_units(preact, half_cols):
    tanh_part = jnp.tanh(preact[:, :half_cols])
    sigmoid_part = jax.nn.sigmoid(preact[:, half_cols:])
    return ((tanh_part * sigmoid_part).astype(jnp.bfloat16), tanh_part, sigmoid_part)


def own_rows(values):
    row_count = values.shape[0] // lax.axis_size("wt")
    return lax.dynamic_slice_in_dim(values, lax.axis_index("wt") * row_count, row_count, 0)


def mixing_short(signal, gated, mix_weight):
    partial_sum = jnp.dot(gated, mix_weight, preferred_element_type=jnp.float32)
    summed = lax.psum(partial_sum, "wt")
    return (signal.astype(jnp.float32) + summed).astype(jnp.bfloat16)


def mixing_long(signal, gated, mix_weight):
    shared = lax.psum_scatter(
        jnp.dot(gated, mix_weight, preferred_element_type=jnp.float32).astype(jnp.bfloat16),
        "wt",
        scatter_dimension=0,
        tiled=True,
    ).astype(jnp.float32)
    return (own_rows(signal).astype(jnp.float32) + shared).astype(jnp.bfloat16)


def gate_grads(upstream, mix_weight, gated, tanh_part, sigmoid_part):
    gated_grad = contract_cols(upstream, mix_weight)
    mix_grad = contract_rows(gated, upstream)
    filter_grad = gated_grad * sigmoid_part * (1.0 - tanh_part * tanh_part)
    gate_grad = gated_grad * tanh_part * sigmoid_part * (1.0 - sigmoid_part)
    return (jnp.concatenate([filter_grad, gate_grad], axis=1).astype(jnp.bfloat16), mix_grad)


def later_short(preact_grad):
    midpoint = preact_grad.shape[0] // 2
    packed = jnp.concatenate([preact_grad[:midpoint], preact_grad], axis=0)
    moved_rows = shifted(packed, "tm", -1)
    later_one = jnp.concatenate([preact_grad[midpoint:], moved_rows[:midpoint]], axis=0)
    return (later_one, moved_rows[midpoint:])


def later_long(preact_grad):
    later_one = shifted(preact_grad, "tm", -1)
    later_two = shifted(preact_grad, "tm", -2)
    return (later_one, later_two)


def finish_layer(
    stacked, preact_grad, later_one, later_two, tap_inputs, mix_grad, upstream, grad_scale
):
    back_sum = contract_cols(preact_grad, stacked[0])
    back_sum = back_sum + contract_cols(later_one, stacked[1])
    back_sum = back_sum + contract_cols(later_two, stacked[2])
    conv_grad = jnp.stack(
        [
            contract_rows(tap_inputs[0], preact_grad),
            contract_rows(tap_inputs[1], preact_grad),
            contract_rows(tap_inputs[2], preact_grad),
        ]
    )
    conv_total, mix_total = (
        lax.psum_scatter(conv_grad, "tm", scatter_dimension=1, tiled=True),
        lax.psum_scatter(mix_grad, "tm", scatter_dimension=1, tiled=True),
    )
    summed = lax.psum(back_sum, "wt")
    lowered = (upstream.astype(jnp.float32) + summed).astype(jnp.bfloat16)
    return (lowered, conv_total * grad_scale, mix_total * grad_scale)


def body(
    signal,
    cotangent,
    first_filter_taps,
    first_gate_taps,
    first_residual_projection,
    second_filter_taps,
    second_gate_taps,
    second_residual_projection,
):
    half_cols = first_filter_taps.shape[2]
    grad_scale = 1.0 / math.sqrt(signal.shape[0] * lax.axis_size("tm"))
    stacked_a = jnp.concatenate([first_filter_taps, first_gate_taps], axis=2)
    stacked_b = jnp.concatenate([second_filter_taps, second_gate_taps], axis=2)
    preact_a, taps_a = preact_short(signal, stacked_a)
    gated_output_first, tanh_branch_first, sigmoid_branch_first = gate_units(preact_a, half_cols)
    hidden_features = mixing_short(signal, gated_output_first, first_residual_projection)
    preact_b, taps_b = preact_long(hidden_features, stacked_b)
    gated_output_second, tanh_branch_second, sigmoid_branch_second = gate_units(preact_b, half_cols)
    second_layer_output = mixing_long(
        hidden_features, gated_output_second, second_residual_projection
    )
    pgrad_b, mixgrad_b = gate_grads(
        cotangent,
        second_residual_projection,
        gated_output_second,
        tanh_branch_second,
        sigmoid_branch_second,
    )
    later_one_b, later_two_b = later_long(pgrad_b)
    hidden_features_gradient, convolution_second_layer, projection_gradient_second = finish_layer(
        stacked_b, pgrad_b, later_one_b, later_two_b, taps_b, mixgrad_b, cotangent, grad_scale
    )
    pgrad_a, mixgrad_a = gate_grads(
        hidden_features_gradient,
        first_residual_projection,
        gated_output_first,
        tanh_branch_first,
        sigmoid_branch_first,
    )
    later_one_a, later_two_a = later_short(pgrad_a)
    input_feature_gradient, convolution_first_layer, projection_gradient_first = finish_layer(
        stacked_a,
        pgrad_a,
        later_one_a,
        later_two_a,
        taps_a,
        mixgrad_a,
        hidden_features_gradient,
        grad_scale,
    )
    return (
        second_layer_output,
        input_feature_gradient,
        convolution_first_layer[:, :, :half_cols],
        convolution_first_layer[:, :, half_cols:],
        projection_gradient_first,
        convolution_second_layer[:, :, :half_cols],
        convolution_second_layer[:, :, half_cols:],
        projection_gradient_second,
    )


def solution(mesh):
    in_specs = (
        P(("grp", "tm"), None),
        P(("grp", "tm"), None),
        P(None, None, "wt"),
        P(None, None, "wt"),
        P("wt", None),
        P(None, None, "wt"),
        P(None, None, "wt"),
        P("wt", None),
    )
    out_specs = (
        P(("grp", "tm", "wt"), None),
        P(("grp", "tm"), None),
        P("grp", "tm", "wt"),
        P("grp", "tm", "wt"),
        P(("grp", "wt"), "tm"),
        P("grp", "tm", "wt"),
        P("grp", "tm", "wt"),
        P(("grp", "wt"), "tm"),
    )
    return jax.shard_map(body, mesh=mesh, in_specs=in_specs, out_specs=out_specs, check_vma=False)
```

profile of v0, /device:TPU:0, one launch (start us, length us, event | category | flops | bytes accessed | tf_op | source)
XLA Modules:
  0.0 455.6 jit_solution(1764214954525177550)
XLA Ops:
  7.2 5.1 %collective-permute-start = (bf16[640,512]{1,0:T(8,128)(2,1)}, bf16[640,512]{1,0:T(8,128)(2,1)S(1)}, u32[]{:S(2)}, u32[]{:S(2)}) collective-permute-start(bf16[640,512]{1,0:T(8,128)(2,1)} %param.8), channel_id=1, source_target_pairs={{0,1},{1,2},{2,3},{4,5},{5,6},{6,7},{8,9},{9,10},{10,11},{12,13},{... | collective-permute-start | bytes 1966088 | tf_op jit(solution)/shard_map/ppermute | solution.py:12
  14.3 12.3 %collective-permute-done = bf16[640,512]{1,0:T(8,128)(2,1)S(1)} collective-permute-done((bf16[640,512]{1,0:T(8,128)(2,1)}, bf16[640,512]{1,0:T(8,128)(2,1)S(1)}, u32[]{:S(2)}, u32[]{:S(2)}) %collective-permute-start) | collective-permute-done | bytes 655392 | tf_op jit(solution)/shard_map/ppermute | solution.py:12
  30.5 41.1 %all-reduce.4.cloned.1.call-done = f32[640,512]{1,0:T(8,128)} async-done(((f32[640,512]{1,0:T(8,128)}), f32[640,512]{1,0:T(8,128)}) %all-reduce.4.cloned.1.call-update) | async-done | bytes 1310736 | tf_op jit(solution)/shard_map/psum | solution.py:62
  71.6 1.6 add_convert_fusion.2
  73.3 3.6 collective-permute-start.1
  76.9 4.3 collective-permute-start.2
  81.9 10.0 %collective-permute-done.1 = bf16[640,512]{1,0:T(8,128)(2,1)S(1)} collective-permute-done((bf16[640,512]{1,0:T(8,128)(2,1)S(1)}, bf16[640,512]{1,0:T(8,128)(2,1)S(1)}, u32[]{:S(2)}, u32[]{:S(2)}) %collective-permute-start.1) | collective-permute-done | bytes 655392 | tf_op jit(solution)/shard_map/ppermute | solution.py:12
  92.8 12.1 %collective-permute-done.2 = bf16[640,512]{1,0:T(8,128)(2,1)S(1)} collective-permute-done((bf16[640,512]{1,0:T(8,128)(2,1)S(1)}, bf16[640,512]{1,0:T(8,128)(2,1)S(1)}, u32[]{:S(2)}, u32[]{:S(2)}) %collective-permute-start.2) | collective-permute-done | bytes 655392 | tf_op jit(solution)/shard_map/ppermute | solution.py:12
  109.5 28.8 %collective-permute-done.3 = bf16[640,512]{0,1:T(8,128)(2,1)S(1)} collective-permute-done((bf16[640,512]{0,1:T(8,128)(2,1)S(1)}, bf16[640,512]{0,1:T(8,128)(2,1)S(1)}, u32[]{:S(2)}, u32[]{:S(2)}) %collective-permute-start.3) | collective-permute-done | bytes 655392 | tf_op jit(solution)/shard_map/ppermute | solution.py:12
  138.9 28.0 %collective-permute-done.4 = bf16[640,512]{0,1:T(8,128)(2,1)S(1)} collective-permute-done((bf16[640,512]{0,1:T(8,128)(2,1)S(1)}, bf16[640,512]{0,1:T(8,128)(2,1)S(1)}, u32[]{:S(2)}, u32[]{:S(2)}) %collective-permute-start.4) | collective-permute-done | bytes 655392 | tf_op jit(solution)/shard_map/ppermute | solution.py:12
  166.9 1.6 convolution_add_fusion.2
  172.1 33.1 %all-reduce.6.cloned.1.call-done = f32[640,512]{1,0:T(8,128)} async-done(((f32[640,512]{1,0:T(8,128)}), f32[640,512]{1,0:T(8,128)}) %all-reduce.6.cloned.1.call-update) | async-done | bytes 1310736 | tf_op jit(solution)/shard_map/psum | solution.py:115
  205.2 1.8 add_convert_fusion.1
  210.9 2.3 copy.24
  214.5 2.1 fusion.22
  216.7 2.6 fusion.11
  219.3 26.4 %collective-permute-done.5 = bf16[960,512]{1,0:T(8,128)(2,1)} collective-permute-done((bf16[960,512]{1,0:T(8,128)(2,1)}, bf16[960,512]{1,0:T(8,128)(2,1)}, u32[]{:S(2)}, u32[]{:S(2)}) %collective-permute-start.5) | collective-permute-done | bytes 983072 | tf_op jit(solution)/shard_map/ppermute | solution.py:12
  245.7 1.7 slice.96
  247.4 1.9 copy.38
  249.3 2.4 convolution_add_fusion.1
  251.7 2.7 convolution_add_fusion
  258.6 1.9 pad_maximum_fusion.1
  261.7 1.6 convolution_bitcast_fusion.5
  264.4 2.0 pad_maximum_fusion
  266.5 1.6 broadcast_multiply_fusion.2
  268.1 1.6 add_convert_fusion.3
  269.7 11.3 %reduce-scatter.10.cloned.1.call-done = f32[256,128]{1,0:T(8,128)} async-done(((f32[256,512]{1,0:T(8,128)}), f32[256,128]{1,0:T(8,128)}) %reduce-scatter.10.cloned.1.call-update) | async-done | bytes 131088 | tf_op jit(solution)/shard_map/reduce_scatter | solution.py:113
  281.0 1.6 broadcast_multiply_fusion.3
  282.5 37.9 %all-reduce.8.cloned.1.call-done = f32[640,512]{1,0:T(8,128)} async-done(((f32[640,512]{1,0:T(8,128)}), f32[640,512]{1,0:T(8,128)}) %all-reduce.8.cloned.1.call-update) | async-done | bytes 1310736 | tf_op jit(solution)/shard_map/psum | solution.py:115
  320.4 2.4 add_convert_fusion
  322.8 60.3 %reduce-scatter.12.cloned.1.call-done = f32[3,128,512]{1,2,0:T(8,128)} async-done(((f32[3,512,512]{1,2,0:T(8,128)}), f32[3,128,512]{1,2,0:T(8,128)}) %reduce-scatter.12.cloned.1.call-update) | async-done | bytes 786448 | tf_op jit(solution)/shard_map/reduce_scatter | solution.py:112
  386.2 59.5 %reduce-scatter.8.cloned.1.call-done = f32[3,128,512]{1,2,0:T(8,128)} async-done(((f32[3,512,512]{1,2,0:T(8,128)}), f32[3,128,512]{1,2,0:T(8,128)}) %reduce-scatter.8.cloned.1.call-update) | async-done | bytes 786448 | tf_op jit(solution)/shard_map/reduce_scatter | solution.py:112
  (109 shorter events, 34.0 us)
Async XLA Ops:
  7.2 98.5 %copy-start = (bf16[256,512]{1,0:T(8,128)(2,1)S(1)}, bf16[256,512]{1,0:T(8,128)(2,1)}, u32[]{:S(2)}) copy-start(bf16[256,512]{1,0:T(8,128)(2,1)} %param.15) | copy-start | bytes 786436
  7.2 6.5 %copy-start.1 = (bf16[640,512]{1,0:T(8,128)(2,1)S(1)}, bf16[640,512]{1,0:T(8,128)(2,1)}, u32[]{:S(2)}) copy-start(bf16[640,512]{1,0:T(8,128)(2,1)} %param.8) | copy-start | bytes 1966084
  7.2 64.4 %all-reduce.4.cloned.1.call-start = ((), (), s32[]{:S(2)}) async-start(), calls=%async_computation.5 | async-start | bytes 2621440 | tf_op jit(solution)/shard_map/psum | solution.py:62
  7.2 6.3 %copy-start.13 = (bf16[3,512,256]{2,1,0:T(8,128)(2,1)S(1)}, bf16[3,512,256]{2,1,0:T(8,128)(2,1)}, u32[]{:S(2)}) copy-start(bf16[3,512,256]{2,1,0:T(8,128)(2,1)} %param.11) | copy-start | bytes 2359300
  7.2 19.4 %collective-permute-start = (bf16[640,512]{1,0:T(8,128)(2,1)}, bf16[640,512]{1,0:T(8,128)(2,1)S(1)}, u32[]{:S(2)}, u32[]{:S(2)}) collective-permute-start(bf16[640,512]{1,0:T(8,128)(2,1)} %param.8), channel_id=1, source_target_pairs={{0,1},{1,2},{2,3},{4,5},{5,6},{6,7},{8,9},{9,10},{10,11},{12,13},{... | collective-permute-start | bytes 1966088 | tf_op jit(solution)/shard_map/ppermute | solution.py:12
  26.6 1.3 copy-start.2
  27.9 1.1 copy-start.26
  29.0 1.4 copy-start.10
  30.5 174.7 %all-reduce.6.cloned.1.call-start = ((), (), s32[]{:S(2)}) async-start(), calls=%async_computation.7 | async-start | bytes 2621440 | tf_op jit(solution)/shard_map/psum | solution.py:115
  71.6 5.2 %copy-start.14 = (bf16[3,512,256]{2,1,0:T(8,128)(2,1)S(1)}, bf16[3,512,256]{2,1,0:T(8,128)(2,1)}, u32[]{:S(2)}) copy-start(bf16[3,512,256]{2,1,0:T(8,128)(2,1)} %param.13) | copy-start | bytes 2359300
  73.2 8.1 %copy-start.6 = (bf16[640,512]{1,0:T(8,128)(2,1)}, bf16[640,512]{1,0:T(8,128)(2,1)S(1)}, u32[]{:S(2)}) copy-start(bf16[640,512]{1,0:T(8,128)(2,1)S(1)} %add_convert_fusion.2) | copy-start | bytes 1966084
  73.2 8.0 %copy-start.15 = (bf16[3,512,256]{2,1,0:T(8,128)(2,1)S(1)}, bf16[3,512,256]{2,1,0:T(8,128)(2,1)}, u32[]{:S(2)}) copy-start(bf16[3,512,256]{2,1,0:T(8,128)(2,1)} %param.14) | copy-start | bytes 2359300
  73.3 18.7 %collective-permute-start.1 = (bf16[640,512]{1,0:T(8,128)(2,1)S(1)}, bf16[640,512]{1,0:T(8,128)(2,1)S(1)}, u32[]{:S(2)}, u32[]{:S(2)}) collective-permute-start(bf16[640,512]{1,0:T(8,128)(2,1)S(1)} %add_convert_fusion.2), channel_id=1, source_target_pairs={{0,1},{1,2},{2,3},{4,5},{5,6},{6,7},{8,9},{9,10},{10,11},{12,13},{... | collective-permute-start | bytes 1966088 | tf_op jit(solution)/shard_map/ppermute | solution.py:12
  76.9 27.9 %collective-permute-start.2 = (bf16[640,512]{1,0:T(8,128)(2,1)S(1)}, bf16[640,512]{1,0:T(8,128)(2,1)S(1)}, u32[]{:S(2)}, u32[]{:S(2)}) collective-permute-start(bf16[640,512]{1,0:T(8,128)(2,1)S(1)} %add_convert_fusion.2), channel_id=1, source_target_pairs={{0,2},{1,3},{4,6},{5,7},{8,10},{9,11},{12,14},{13,15},{16,18},{17,... | collective-permute-start | bytes 1966088 | tf_op jit(solution)/shard_map/ppermute | solution.py:12
  92.8 12.9 %copy-start.11 = (bf16[640,512]{1,0:T(8,128)(2,1)S(1)}, bf16[640,512]{1,0:T(8,128)(2,1)}, u32[]{:S(2)}) copy-start(bf16[640,512]{1,0:T(8,128)(2,1)} %param.9) | copy-start | bytes 1966084
  106.3 3.2 copy-start.20
  106.3 3.2 copy-start.23
  106.4 32.0 %collective-permute-start.3 = (bf16[640,512]{0,1:T(8,128)(2,1)S(1)}, bf16[640,512]{0,1:T(8,128)(2,1)S(1)}, u32[]{:S(2)}, u32[]{:S(2)}) collective-permute-start(bf16[640,512]{0,1:T(8,128)(2,1)S(1)} %pad_maximum_fusion.4), channel_id=1, source_target_pairs={{1,0},{2,1},{3,2},{5,4},{6,5},{7,6},{9,8},{10,9},{11,10},{13,12},{... | collective-permute-start | bytes 1966088 | tf_op jit(solution)/shard_map/ppermute | solution.py:12
  107.7 59.2 %collective-permute-start.4 = (bf16[640,512]{0,1:T(8,128)(2,1)S(1)}, bf16[640,512]{0,1:T(8,128)(2,1)S(1)}, u32[]{:S(2)}, u32[]{:S(2)}) collective-permute-start(bf16[640,512]{0,1:T(8,128)(2,1)S(1)} %pad_maximum_fusion.4), channel_id=1, source_target_pairs={{2,0},{3,1},{6,4},{7,5},{10,8},{11,9},{14,12},{15,13},{18,16},{19,... | collective-permute-start | bytes 1966088 | tf_op jit(solution)/shard_map/ppermute | solution.py:12
  168.5 98.0 %reduce-scatter.14.cloned.1.call-start = ((), (), s32[]{:S(2)}) async-start(), calls=%async_computation.12 | async-start | bytes 655360 | tf_op jit(solution)/shard_map/reduce_scatter | solution.py:113
  170.8 97.3 %reduce-scatter.6.cloned.1.call-start = ((), (), s32[]{:S(2)}) async-start(), calls=%async_computation.6 | async-start | bytes 819200 | tf_op jit(solution)/shard_map/reduce_scatter | solution.py:67
  172.0 108.9 %reduce-scatter.10.cloned.1.call-start = ((), (), s32[]{:S(2)}) async-start(), calls=%async_computation.10 | async-start | bytes 655360 | tf_op jit(solution)/shard_map/reduce_scatter | solution.py:113
  205.2 1.9 copy-start.5
  213.2 32.5 %collective-permute-start.5 = (bf16[960,512]{1,0:T(8,128)(2,1)}, bf16[960,512]{1,0:T(8,128)(2,1)}, u32[]{:S(2)}, u32[]{:S(2)}) collective-permute-start(bf16[960,512]{1,0:T(8,128)(2,1)} %copy.24), channel_id=1, source_target_pairs={{1,0},{2,1},{3,2},{5,4},{6,5},{7,6},{9,8},{10,9},{11,10},{13,12},{... | collective-permute-start | bytes 2949128 | tf_op jit(solution)/shard_map/ppermute | solution.py:12
  216.6 103.8 %all-reduce.8.cloned.1.call-start = ((), (), s32[]{:S(2)}) async-start(), calls=%async_computation.8 | async-start | bytes 2621440 | tf_op jit(solution)/shard_map/psum | solution.py:115
  254.4 1.2 copy-start.21
  254.4 1.3 copy-start.24
  254.4 128.6 %reduce-scatter.12.cloned.1.call-start = ((), (), s32[]{:S(2)}) async-start(), calls=%async_computation.11 | async-start | bytes 3932160 | tf_op jit(solution)/shard_map/reduce_scatter | solution.py:112
  255.7 1.2 copy-start.22
  255.7 1.3 copy-start.25
  260.6 185.1 %reduce-scatter.8.cloned.1.call-start = ((), (), s32[]{:S(2)}) async-start(), calls=%async_computation.9 | async-start | bytes 3932160 | tf_op jit(solution)/shard_map/reduce_scatter | solution.py:112
  261.7 1.6 copy-start.9
  (9 other events, 9.2 us)
Sparse Core Ops, SparseCore 0:
  30.6 40.9 all-reduce.3
  168.6 36.4 all-reduce.5
  207.4 24.6 reduce-scatter.13
  235.1 21.9 reduce-scatter.5
  259.3 21.6 reduce-scatter.9
  283.2 37.1 all-reduce.7
  322.7 60.2 reduce-scatter.11
  385.4 60.2 reduce-scatter.7
where the time goes:
time: 457 us; the launch traced here: 456 us
  waiting for transfers between devices  361 us (79%)
  matrix products  26.6 us (6%)
  other arithmetic  19.5 us (4%)
  starting transfers between devices  17.4 us (4%)
  local copies, waits for them, and re-layouts  16.7 us (4%)
  between operations  14.5 us (3%)
    reduce_scatter x2, waiting for transfers between devices, finish_layer(): lax.psum_scatter(conv_grad, 'tm', scatter_dimension=1, tiled=True)  120 us
    ppermute x6, waiting for transfers between devices, shifted(): return lax.ppermute(block, axis, route)  118 us
    psum x2, waiting for transfers between devices, finish_layer(): summed = lax.psum(back_sum, 'wt')  71 us
    psum x1, waiting for transfers between devices, mixing_short(): summed = lax.psum(partial_sum, 'wt')  41.1 us
    ppermute x6, starting transfers between devices, shifted(): return lax.ppermute(block, axis, route)  16.8 us
    unnamed x61, local copies, waits for them, and re-layouts  12.5 us
    dot_general x8, matrix products, contract_cols(): lax.dot_general(left_side, right_side, (((1,), (1,)), ((), ())), preferre...  12.5 us
    reduce_scatter x2, waiting for transfers between devices, finish_layer(): lax.psum_scatter(mix_grad, 'tm', scatter_dimension=1, tiled=True)  11.3 us
  transfers between devices with their start and end apart: 14, of which 12 were waited for; matrix products, arithmetic and copies ran while one was open for 10% of the time, Pallas kernels for 0%

commit v1 on v0

--- a/solution.py
+++ b/solution.py
@@ -1,8 +1,11 @@
+import functools
 import math
 
 import jax
 import jax.numpy as jnp
 from jax import lax
+from jax.experimental import pallas as pl
+from jax.experimental.pallas import tpu as pltpu
 from jax.sharding import PartitionSpec as P
 
 
@@ -180,6 +183,430 @@
     )
 
 
+def fused_kernel(
+    tm, scale,
+    sig, cot, f1, g1, m1, f2, g2, m2,
+    o_out2, o_gx, o_cf1, o_cg1, o_mg1, o_cf2, o_cg2, o_mg2,
+    sj, hj, w1, w2, a1, b1, gt1, a2, b2, gt2, gg, pre, pg1, pg2, hg, gxs,
+    a_snd, a_rcv, b_snd, b_rcv, own, r_snd, r_rcv,
+    w_snd, w_rcv, w_own, m_snd, m_rcv, m_own,
+    load_sem, as_sem, ar_sem, bs_sem, br_sem, gs_sem, gr_sem,
+    zs_sem, zr_sem, ws_sem, wr_sem, ms_sem, mr_sem,
+):
+    seg, chans = sig.shape
+    quarter = seg // 4
+    half_seg = seg // 2
+    cols = f1.shape[2]
+    cblk = chans // tm
+    bf16, f32 = jnp.bfloat16, jnp.float32
+    w = lax.axis_index("wt")
+    z = lax.axis_index("tm")
+    x, c = w // 2, w % 2
+    mate = 2 * x + (1 - c)
+    across = 2 * (1 - x) + c
+    diag = 2 * (1 - x) + (1 - c)
+
+    def rows(q, base=0):
+        return pl.ds(pl.multiple_of(base + q * quarter, quarter), quarter)
+
+    def dot(l, r):
+        return jnp.dot(l, r, preferred_element_type=f32)
+
+    def dot_t(l, r):
+        return lax.dot_general(l, r, (((1,), (1,)), ((), ())), preferred_element_type=f32)
+
+    def dot_rows(l, r):
+        return lax.dot_general(l, r, (((0,), (0,)), ((), ())), preferred_element_type=f32)
+
+    pending = []
+
+    def remote(src, dst, ssem, rsem, target):
+        return pltpu.make_async_remote_copy(
+            src_ref=src, dst_ref=dst, send_sem=ssem, recv_sem=rsem,
+            device_id=target, device_id_type=pl.DeviceIdType.MESH,
+        )
+
+    def go(copy, cond=None):
+        pending.append((copy, cond))
+        if cond is None:
+            copy.start()
+        else:
+            pl.when(cond)(copy.start)
+
+    def when(cond, fn):
+        if cond is None:
+            fn()
+        else:
+            pl.when(cond)(fn)
+
+    loads = []
+    for n, (layer, fil, gat) in enumerate(((w1, f1, g1), (w2, f2, g2))):
+        for m, part in enumerate((fil, gat)):
+            loads.append(
+                pltpu.make_async_copy(
+                    part, layer.at[:, :, m * cols : (m + 1) * cols], load_sem.at[2 * n + m]
+                )
+            )
+    for load in loads:
+        load.start()
+
+    barrier = pltpu.get_barrier_semaphore()
+    for peer in (mate, across):
+        pl.semaphore_signal(
+            barrier, inc=1, device_id={"wt": peer}, device_id_type=pl.DeviceIdType.MESH
+        )
+    for d in range(1, tm):
+        pl.semaphore_signal(
+            barrier, inc=1, device_id={"tm": lax.rem(z + d, tm)},
+            device_id_type=pl.DeviceIdType.MESH,
+        )
+    pl.semaphore_wait(barrier, 2 + tm - 1)
+
+    class Gather:
+        def __init__(self, n, buf, base, cond=None):
+            self.cond = cond
+            mine, theirs = buf.at[rows(w, base)], buf.at[rows(across, base)]
+            self.cross = remote(mine, mine, gs_sem.at[n, 0], gr_sem.at[n, 0], {"wt": across})
+            self.near = remote(mine, mine, gs_sem.at[n, 1], gr_sem.at[n, 1], {"wt": mate})
+            self.fwd = remote(theirs, theirs, gs_sem.at[n, 2], gr_sem.at[n, 2], {"wt": mate})
+
+        def start(self):
+            go(self.cross, self.cond)
+            go(self.near, self.cond)
+
+        def forward(self):
+            when(self.cond, self.cross.wait_recv)
+            go(self.fwd, self.cond)
+
+        def finish(self):
+            when(self.cond, self.near.wait_recv)
+            when(self.cond, self.fwd.wait_recv)
+
+    def a_copy(n, j):
+        return remote(
+            a_snd.at[n, j], a_rcv.at[n, j], as_sem.at[n, j], ar_sem.at[n, j], {"wt": mate}
+        )
+
+    def b_copy(n):
+        return remote(b_snd.at[n], b_rcv.at[n], bs_sem.at[n], br_sem.at[n], {"wt": across})
+
+    def rs_start(n, fn):
+        for j, q in enumerate((diag, mate)):
+            a_snd[n, j] = fn(q).astype(bf16)
+            go(a_copy(n, j))
+        for j, q in enumerate((across, w)):
+            own[n, j] = fn(q)
+
+    def rs_mid(n):
+        a_copy(n, 0).wait_recv()
+        b_snd[n] = (own[n, 0] + a_rcv[n, 0].astype(f32)).astype(bf16)
+        go(b_copy(n))
+
+    def rs_end(n):
+        a_copy(n, 1).wait_recv()
+        b_copy(n).wait_recv()
+        return own[n, 1] + a_rcv[n, 1].astype(f32) + b_rcv[n].astype(f32)
+
+    def z_copy(n, src, dst, step):
+        return remote(
+            src, dst, zs_sem.at[n], zr_sem.at[n], {"tm": lax.rem(z + step + tm, tm)}
+        )
+
+    halo = z_copy(0, sig.at[rows(w)], sj.at[rows(w)], 1)
+    go(halo, z < tm - 1)
+    sj[seg : 2 * seg] = sig[...]
+
+    @pl.when(z == 0)
+    def _():
+        sj[0:seg] = jnp.zeros((seg, chans), bf16)
+        hj[seg : 2 * seg] = jnp.zeros((seg, chans), bf16)
+
+    @pl.when(z < 2)
+    def _():
+        hj[0:seg] = jnp.zeros((seg, chans), bf16)
+
+    @pl.loop(0, 4)
+    def _(r):
+        gg[rows(r), :] = dot_t(cot[rows(r), :], m2[...])
+
+    pl.when(z > 0)(halo.wait_recv)
+    sig_gather = Gather(0, sj, 0, z > 0)
+    sig_gather.start()
+    loads[0].wait()
+    loads[1].wait()
+
+    @pl.loop(0, 4)
+    def _(r):
+        pre[rows(r), :] = dot(sj[rows(r, seg), :], w1[0])
+
+    sig_gather.forward()
+    sig_gather.finish()
+
+    def gate(p, a_ref, b_ref, g_ref, q):
+        a = jnp.tanh(p[:, :cols])
+        b = jax.nn.sigmoid(p[:, cols:])
+        a_ref[rows(q), :] = a
+        b_ref[rows(q), :] = b
+        g = (a * b).astype(bf16)
+        g_ref[rows(q), :] = g
+        return a, b, g
+
+    def first_quarter(q):
+        p = pre[rows(q), :] + dot(sj[rows(q, half_seg), :], w1[1]) + dot(sj[rows(q), :], w1[2])
+        g = gate(p, a1, b1, gt1, q)[2]
+        return dot(g, m1[...])
+
+    rs_start(0, first_quarter)
+    rs_mid(0)
+    hj[rows(w, 2 * seg), :] = (sig[rows(w), :].astype(f32) + rs_end(0)).astype(bf16)
+
+    g_own = Gather(1, hj, 2 * seg)
+    one = z_copy(1, hj.at[rows(w, 2 * seg)], hj.at[rows(w, seg)], 1)
+    two = z_copy(2, hj.at[rows(w, 2 * seg)], hj.at[rows(w)], 2)
+    g_own.start()
+    go(one, z < tm - 1)
+    go(two, z < tm - 2)
+    g_own.forward()
+    pl.when(z > 0)(one.wait_recv)
+    g_one = Gather(2, hj, seg, z > 0)
+    g_one.start()
+    g_own.finish()
+    loads[2].wait()
+    loads[3].wait()
+
+    @pl.loop(0, 4)
+    def _(r):
+        pre[rows(r), :] = dot(hj[rows(r, 2 * seg), :], w2[0])
+
+    g_one.forward()
+    pl.when(z > 1)(two.wait_recv)
+    g_two = Gather(3, hj, 0, z > 1)
+    g_two.start()
+    g_one.finish()
+
+    @pl.loop(0, 4)
+    def _(r):
+        pre[rows(r), :] += dot(hj[rows(r, seg), :], w2[1])
+
+    g_two.forward()
+    g_two.finish()
+
+    def pre_grad(gval, a, b, pg, q):
+        pg[rows(q), 0:cols] = (gval * b * (1.0 - a * a)).astype(bf16)
+        pg[rows(q), cols : 2 * cols] = (gval * a * b * (1.0 - b)).astype(bf16)
+
+    @pl.loop(0, 4)
+    def _(r):
+        p = pre[rows(r), :] + dot(hj[rows(r), :], w2[2])
+        a, b, _ = gate(p, a2, b2, gt2, r)
+        pre_grad(gg[rows(r), :], a, b, pg2, r)
+
+    rs_start(1, lambda q: dot_t(pg2[rows(q), :], w2[2]))
+    rs_start(2, lambda q: dot_t(pg2[rows(q), :], w2[1]))
+    rs_mid(1)
+    rs_start(3, lambda q: dot_t(pg2[rows(q), :], w2[0]))
+    rs_mid(2)
+    rs_mid(3)
+
+    def weight_blocks(n, taps, base, spread, pg, gated, up, d):
+        j = lax.rem(z + d, tm)
+        at = pl.ds(pl.multiple_of(j * cblk, cblk), cblk)
+        for k in range(3):
+            lo = base - spread * k
+            block = dot_rows(taps[lo : lo + seg, at], pg[...])
+            if d == 0:
+                w_own[n, k * cblk : (k + 1) * cblk, :] = block
+            else:
+                w_snd[n, d - 1, k * cblk : (k + 1) * cblk, :] = block.astype(bf16)
+        mix = dot_rows(gated[...], up[:, at])
+        if d == 0:
+            m_own[n] = mix
+        else:
+            m_snd[n, d - 1] = mix.astype(bf16)
+
+    def w_copies(n, d):
+        target = {"tm": lax.rem(z + d, tm)}
+        s = d - 1
+        return (
+            remote(w_snd.at[n, s], w_rcv.at[n, s], ws_sem.at[n, s], wr_sem.at[n, s], target),
+            remote(m_snd.at[n, s], m_rcv.at[n, s], ms_sem.at[n, s], mr_sem.at[n, s], target),
+        )
+
+    def weight_send(n, d):
+        for copy in w_copies(n, d):
+            go(copy)
+
+    def weight_finish(n, o_f, o_g, o_m):
+        for d in range(1, tm):
+            for copy in w_copies(n, d):
+                copy.wait_recv()
+        for k in range(3):
+            at = slice(k * cblk, (k + 1) * cblk)
+            total = w_own[n, at, :]
+            for d in range(1, tm):
+                total = total + w_rcv[n, d - 1, at, :].astype(f32)
+            total = total * scale
+            o_f[k] = total[:, :cols]
+            o_g[k] = total[:, cols:]
+        total = m_own[n]
+        for d in range(1, tm):
+            total = total + m_rcv[n, d - 1].astype(f32)
+        o_m[...] = total * scale
+
+    second = (1, hj, 2 * seg, seg, pg2, gt2, cot)
+    weight_blocks(*second, 1)
+    r_snd[0] = rs_end(1).astype(bf16)
+    back_two = z_copy(3, r_snd.at[0], r_rcv.at[0], -2)
+    go(back_two, z > 1)
+    r_snd[1] = rs_end(2).astype(bf16)
+    back_one = z_copy(4, r_snd.at[1], r_rcv.at[1], -1)
+    go(back_one, z > 0)
+    weight_send(1, 1)
+    for d in range(2, tm):
+        weight_blocks(*second, d)
+        weight_send(1, d)
+    total = cot[rows(w), :].astype(f32) + rs_end(3)
+    own[3, 0] = total
+
+    @pl.when(z < tm - 1)
+    def _():
+        back_one.wait_recv()
+        own[3, 0] += r_rcv[1].astype(f32)
+
+    @pl.when(z < tm - 2)
+    def _():
+        back_two.wait_recv()
+        own[3, 0] += r_rcv[0].astype(f32)
+
+    hg[rows(w), :] = own[3, 0].astype(bf16)
+    g_hg = Gather(4, hg, 0)
+    g_hg.start()
+    rs_start(4, lambda q: dot(gt2[rows(q), :], m2[...]))
+    g_hg.forward()
+    g_hg.finish()
+
+    @pl.loop(0, 4)
+    def _(r):
+        gval = dot_t(hg[rows(r), :], m1[...])
+        pre_grad(gval, a1[rows(r), :], b1[rows(r), :], pg1, r)
+
+    def to_earlier(q):
+        late = (q >= 2).astype(f32)
+        shifted_q = lax.rem(q + 2, 4)
+        return dot_t(pg1[rows(q), :], w1[2]) + late * dot_t(pg1[rows(shifted_q), :], w1[1])
+
+    def to_here(q):
+        early = (q < 2).astype(f32)
+        shifted_q = lax.rem(q + 2, 4)
+        return dot_t(pg1[rows(q), :], w1[0]) + early * dot_t(pg1[rows(shifted_q), :], w1[1])
+
+    rs_start(5, to_earlier)
+    rs_mid(5)
+    rs_start(6, to_here)
+    rs_mid(6)
+    rs_mid(4)
+    first = (0, sj, seg, half_seg, pg1, gt1, hg)
+    weight_blocks(*first, 1)
+    r_snd[2] = rs_end(5).astype(bf16)
+    back_first = z_copy(5, r_snd.at[2], r_rcv.at[2], -1)
+    go(back_first, z > 0)
+    weight_send(0, 1)
+    for d in range(2, tm):
+        weight_blocks(*first, d)
+        weight_send(0, d)
+    own[6, 0] = hg[rows(w), :].astype(f32) + rs_end(6)
+
+    @pl.when(z < tm - 1)
+    def _():
+        back_first.wait_recv()
+        own[6, 0] += r_rcv[2].astype(f32)
+
+    gxs[rows(w), :] = own[6, 0].astype(bf16)
+    g_gx = Gather(5, gxs, 0)
+    g_gx.start()
+    weight_blocks(*second, 0)
+    g_gx.forward()
+    weight_blocks(*first, 0)
+    o_out2[...] = (hj[rows(w, 2 * seg), :].astype(f32) + rs_end(4)).astype(bf16)
+    g_gx.finish()
+    o_gx[...] = gxs[...]
+    weight_finish(1, o_cf2, o_cg2, o_mg2)
+    weight_finish(0, o_cf1, o_cg1, o_mg1)
+    for copy, cond in pending:
+        when(cond, copy.wait_send)
+
+
+def fused_body(*args):
+    sig, cot, f1 = args[:3]
+    seg, chans = sig.shape
+    cols = f1.shape[2]
+    tm = lax.axis_size("tm")
+    quarter, cblk = seg // 4, chans // tm
+    bf16, f32 = jnp.bfloat16, jnp.float32
+    scale = 1.0 / math.sqrt(seg * tm)
+    vm = pltpu.VMEM
+    dma = pltpu.SemaphoreType.DMA
+    wide, others = 2 * cols, tm - 1
+    scratch = [
+        vm((2 * seg, chans), bf16),
+        vm((3 * seg, chans), bf16),
+        vm((3, chans, wide), bf16),
+        vm((3, chans, wide), bf16),
+        vm((seg, cols), f32),
+        vm((seg, cols), f32),
+        vm((seg, cols), bf16),
+        vm((seg, cols), f32),
+        vm((seg, cols), f32),
+        vm((seg, cols), bf16),
+        vm((seg, cols), f32),
+        vm((seg, wide), f32),
+        vm((seg, wide), bf16),
+        vm((seg, wide), bf16),
+        vm((seg, chans), bf16),
+        vm((seg, chans), bf16),
+        vm((7, 2, quarter, chans), bf16),
+        vm((7, 2, quarter, chans), bf16),
+        vm((7, quarter, chans), bf16),
+        vm((7, quarter, chans), bf16),
+        vm((7, 2, quarter, chans), f32),
+        vm((3, quarter, chans), bf16),
+        vm((3, quarter, chans), bf16),
+        vm((2, others, 3 * cblk, wide), bf16),
+        vm((2, others, 3 * cblk, wide), bf16),
+        vm((2, 3 * cblk, wide), f32),
+        vm((2, others, cols, cblk), bf16),
+        vm((2, others, cols, cblk), bf16),
+        vm((2, cols, cblk), f32),
+        dma((4,)),
+        dma((7, 2)), dma((7, 2)), dma((7,)), dma((7,)),
+        dma((6, 3)), dma((6, 3)),
+        dma((6,)), dma((6,)),
+        dma((2, others)), dma((2, others)), dma((2, others)), dma((2, others)),
+    ]
+    conv = jax.ShapeDtypeStruct((3, cblk, cols), f32)
+    mix = jax.ShapeDtypeStruct((cols, cblk), f32)
+    in_vm = pl.BlockSpec(memory_space=pltpu.VMEM)
+    in_any = pl.BlockSpec(memory_space=pl.ANY)
+    return pl.pallas_call(
+        functools.partial(fused_kernel, tm, scale),
+        out_shape=(
+            jax.ShapeDtypeStruct((quarter, chans), bf16),
+            jax.ShapeDtypeStruct((seg, chans), bf16),
+            conv, conv, mix, conv, conv, mix,
+        ),
+        in_specs=[in_vm, in_vm, in_any, in_any, in_vm, in_any, in_any, in_vm],
+        out_specs=(in_vm,) * 8,
+        scratch_shapes=scratch,
+        compiler_params=pltpu.CompilerParams(
+            collective_id=0, has_side_effects=True, vmem_limit_bytes=56 * 1024 * 1024
+        ),
+    )(*args)
+
+
+def fits(mesh):
+    return mesh.shape["wt"] == 4 and 3 <= mesh.shape["tm"] <= 4
+
+
 def solution(mesh):
     in_specs = (
         P(("grp", "tm"), None),
@@ -201,4 +628,4 @@
         P("grp", "tm", "wt"),
         P(("grp", "wt"), "tm"),
     )
-    return jax.shard_map(body, mesh=mesh, in_specs=in_specs, out_specs=out_specs, check_vma=False)
+    return jax.shard_map(fused_body if fits(mesh) else body, mesh=mesh, in_specs=in_specs, out_specs=out_specs, check_vma=False)

time: 457 us -> 155 us (0.34)
  the two profiles are of different devices: /device:TPU:0 before, /device:TPU:9 now
where the time goes in v1:
time: 155 us
  Pallas kernels  145 us (94%)
  local copies, waits for them, and re-layouts  9.22 us (6%)
    pallas_call x1, Pallas kernels, fused_body(): pl.pallas_call(functools.partial(fused_kernel, tm, scale), out_shape=(jax...  145 us
    unnamed x20, local copies, waits for them, and re-layouts  9.22 us

profile of v1, /device:TPU:9, one launch (start us, length us, event | category | flops | bytes accessed | tf_op | source)
XLA Modules:
  0.0 155.0 jit_solution(14199643982052928029)
XLA Ops:
  0.6 145.2 %shard_map.143 = (bf16[160,512]{1,0:T(8,128)(2,1)}, bf16[640,512]{1,0:T(8,128)(2,1)}, f32[3,128,256]{2,1,0:T(8,128)}, f32[3,128,256]{2,1,0:T(8,128)}, f32[256,12...) custom-call(bf16[640,512]{1,0:T(8,128)(2,1)} %sig.1, bf16[640,512]{1,0:T(8,128)(2,1)} %cot.1, ...), custom_call_target="tpu_custom_call" | custom-call | tf_op jit(solution)/shard_map/pallas_call | solution.py:590
  145.8 1.6 %copy.24 = bf16[160,512]{1,0:T(8,128)(2,1)} copy(bf16[160,512]{1,0:T(8,128)(2,1)} %get-tuple-element.16) | data formatting | bytes 327680
  147.4 0.0 copy-start.3
  147.4 2.0 %copy.25 = bf16[640,512]{1,0:T(8,128)(2,1)} copy(bf16[640,512]{1,0:T(8,128)(2,1)} %get-tuple-element.17) | data formatting | bytes 1310720
  149.4 0.0 copy-done.3
  149.4 0.0 copy-start.2
  149.4 0.7 copy.26
  150.2 0.4 copy-done.2
  150.6 0.0 copy-start.5
  150.6 0.0 copy-start.1
  150.6 0.7 copy.27
  151.3 0.2 copy-done.5
  151.6 0.7 copy.28
  152.2 0.0 copy-done.1
  152.2 0.0 copy-start
  152.2 0.7 copy.29
  153.0 0.4 copy-done
  153.4 0.0 copy-start.4
  153.4 0.7 copy.30
  154.1 0.3 copy-done.4
  154.4 0.7 copy.31
Async XLA Ops:
  147.4 2.0 %copy-start.3 = (f32[3,128,256]{2,1,0:T(8,128)S(1)}, f32[3,128,256]{2,1,0:T(8,128)}, u32[]{:S(2)}) copy-start(f32[3,128,256]{2,1,0:T(8,128)} %get-tuple-element.18) | copy-start | bytes 1179652
  149.4 1.1 copy-start.2
  150.6 1.0 copy-start.5
  150.6 1.7 %copy-start.1 = (f32[3,128,256]{2,1,0:T(8,128)S(1)}, f32[3,128,256]{2,1,0:T(8,128)}, u32[]{:S(2)}) copy-start(f32[3,128,256]{2,1,0:T(8,128)} %get-tuple-element.21) | copy-start | bytes 1179652
  152.2 1.1 copy-start
  153.4 1.0 copy-start.4

commit v2 on v1

--- a/solution.py
+++ b/solution.py
@@ -189,7 +189,7 @@
     o_out2, o_gx, o_cf1, o_cg1, o_mg1, o_cf2, o_cg2, o_mg2,
     sj, hj, w1, w2, a1, b1, gt1, a2, b2, gt2, gg, pre, pg1, pg2, hg, gxs,
     a_snd, a_rcv, b_snd, b_rcv, own, r_snd, r_rcv,
-    w_snd, w_rcv, w_own, m_snd, m_rcv, m_own,
+    w_snd, w_rcv, w_own, w_far, m_snd, m_rcv, m_own, m_far,
     load_sem, as_sem, ar_sem, bs_sem, br_sem, gs_sem, gr_sem,
     zs_sem, zr_sem, ws_sem, wr_sem, ms_sem, mr_sem,
 ):
@@ -312,6 +312,9 @@
             src, dst, zs_sem.at[n], zr_sem.at[n], {"tm": lax.rem(z + step + tm, tm)}
         )
 
+    def inner_of(i):
+        return jnp.logical_and(i > 0, i < tm - 1)
+
     halo = z_copy(0, sig.at[rows(w)], sj.at[rows(w)], 1)
     go(halo, z < tm - 1)
     sj[seg : 2 * seg] = sig[...]
@@ -362,12 +365,12 @@
 
     g_own = Gather(1, hj, 2 * seg)
     one = z_copy(1, hj.at[rows(w, 2 * seg)], hj.at[rows(w, seg)], 1)
-    two = z_copy(2, hj.at[rows(w, 2 * seg)], hj.at[rows(w)], 2)
+    two = z_copy(2, hj.at[rows(w, seg)], hj.at[rows(w)], 1)
     g_own.start()
     go(one, z < tm - 1)
-    go(two, z < tm - 2)
     g_own.forward()
     pl.when(z > 0)(one.wait_recv)
+    go(two, inner_of(z))
     g_one = Gather(2, hj, seg, z > 0)
     g_one.start()
     g_own.finish()
@@ -408,75 +411,123 @@
     rs_mid(2)
     rs_mid(3)
 
-    def weight_blocks(n, taps, base, spread, pg, gated, up, d):
-        j = lax.rem(z + d, tm)
+    low = z < 2
+    inner = inner_of(z)
+    outer = jnp.logical_not(inner)
+    far_end = jnp.where(low, tm - 1, 0)
+    block_of = (
+        far_end,
+        jnp.where(low, 2, 1),
+        jnp.where(z == 0, 1, jnp.where(z == 1, 0, jnp.where(z == 2, 3, 2))),
+        z,
+    )
+    target_of = (
+        jnp.where(z == 0, 1, jnp.where(z == tm - 1, 2, far_end)), block_of[1], block_of[2]
+    )
+    middle_slot = jnp.where(inner, 2, 3)
+    land_of = (0, middle_slot, 1)
+
+    def weight_blocks(n, taps, base, spread, pg, gated, up, slot):
+        j = block_of[slot]
         at = pl.ds(pl.multiple_of(j * cblk, cblk), cblk)
+        mix = dot_rows(gated[...], up[:, at])
+        if slot == 0:
+            m_far[n] = mix
+        if slot == 3:
+            m_own[n] = mix
+        else:
+            m_snd[n, slot] = mix.astype(bf16)
         for k in range(3):
             lo = base - spread * k
             block = dot_rows(taps[lo : lo + seg, at], pg[...])
-            if d == 0:
+            if slot == 0:
+                w_far[n, k * cblk : (k + 1) * cblk, :] = block
+            if slot == 3:
                 w_own[n, k * cblk : (k + 1) * cblk, :] = block
             else:
-                w_snd[n, d - 1, k * cblk : (k + 1) * cblk, :] = block.astype(bf16)
-        mix = dot_rows(gated[...], up[:, at])
-        if d == 0:
-            m_own[n] = mix
-        else:
-            m_snd[n, d - 1] = mix.astype(bf16)
-
-    def w_copies(n, d):
-        target = {"tm": lax.rem(z + d, tm)}
-        s = d - 1
+                w_snd[n, slot, k * cblk : (k + 1) * cblk, :] = block.astype(bf16)
+
+    def w_copies(n, slot, land):
+        target = {"tm": target_of[slot]}
         return (
-            remote(w_snd.at[n, s], w_rcv.at[n, s], ws_sem.at[n, s], wr_sem.at[n, s], target),
-            remote(m_snd.at[n, s], m_rcv.at[n, s], ms_sem.at[n, s], mr_sem.at[n, s], target),
+            remote(
+                w_snd.at[n, slot], w_rcv.at[n, land], ws_sem.at[n, slot], wr_sem.at[n, land], target
+            ),
+            remote(
+                m_snd.at[n, slot], m_rcv.at[n, land], ms_sem.at[n, slot], mr_sem.at[n, land], target
+            ),
         )
 
-    def weight_send(n, d):
-        for copy in w_copies(n, d):
-            go(copy)
+    def weight_send(n, slot):
+        for copy in w_copies(n, slot, land_of[slot]):
+            if slot > 0:
+                go(copy)
+            else:
+                go(copy, outer)
+
+    def weight_relay(n):
+        copies = w_copies(n, 0, 0)
+
+        @pl.when(inner)
+        def _():
+            for copy in copies:
+                copy.wait_recv()
+            w_snd[n, 0] = (w_far[n] + w_rcv[n, 0].astype(f32)).astype(bf16)
+            m_snd[n, 0] = (m_far[n] + m_rcv[n, 0].astype(f32)).astype(bf16)
+
+        for copy in copies:
+            go(copy, inner)
 
     def weight_finish(n, o_f, o_g, o_m):
-        for d in range(1, tm):
-            for copy in w_copies(n, d):
+        def take(land):
+            for copy in w_copies(n, 0, land):
                 copy.wait_recv()
+            w_own[n] += w_rcv[n, land].astype(f32)
+            m_own[n] += m_rcv[n, land].astype(f32)
+
+        take(1)
+
+        @pl.when(inner)
+        def _():
+            take(2)
+            take(3)
+
+        @pl.when(outer)
+        def _():
+            take(0)
+
         for k in range(3):
-            at = slice(k * cblk, (k + 1) * cblk)
-            total = w_own[n, at, :]
-            for d in range(1, tm):
-                total = total + w_rcv[n, d - 1, at, :].astype(f32)
-            total = total * scale
+            total = w_own[n, k * cblk : (k + 1) * cblk, :] * scale
             o_f[k] = total[:, :cols]
             o_g[k] = total[:, cols:]
-        total = m_own[n]
-        for d in range(1, tm):
-            total = total + m_rcv[n, d - 1].astype(f32)
-        o_m[...] = total * scale
+        o_m[...] = m_own[n] * scale
 
     second = (1, hj, 2 * seg, seg, pg2, gt2, cot)
+    weight_blocks(*second, 0)
+    r_snd[0] = rs_end(1).astype(bf16)
+    back_two = z_copy(3, r_snd.at[0], r_rcv.at[0], -1)
+    go(back_two, z > 1)
     weight_blocks(*second, 1)
-    r_snd[0] = rs_end(1).astype(bf16)
-    back_two = z_copy(3, r_snd.at[0], r_rcv.at[0], -2)
-    go(back_two, z > 1)
-    r_snd[1] = rs_end(2).astype(bf16)
+    own[2, 0] = rs_end(2)
+
+    @pl.when(inner_of(z))
+    def _():
+        back_two.wait_recv()
+        own[2, 0] += r_rcv[0].astype(f32)
+
+    r_snd[1] = own[2, 0].astype(bf16)
     back_one = z_copy(4, r_snd.at[1], r_rcv.at[1], -1)
     go(back_one, z > 0)
+    weight_send(1, 0)
     weight_send(1, 1)
-    for d in range(2, tm):
-        weight_blocks(*second, d)
-        weight_send(1, d)
-    total = cot[rows(w), :].astype(f32) + rs_end(3)
-    own[3, 0] = total
+    weight_blocks(*second, 2)
+    weight_send(1, 2)
+    own[3, 0] = cot[rows(w), :].astype(f32) + rs_end(3)
 
     @pl.when(z < tm - 1)
     def _():
         back_one.wait_recv()
         own[3, 0] += r_rcv[1].astype(f32)
-
-    @pl.when(z < tm - 2)
-    def _():
-        back_two.wait_recv()
-        own[3, 0] += r_rcv[0].astype(f32)
 
     hg[rows(w), :] = own[3, 0].astype(bf16)
     g_hg = Gather(4, hg, 0)
@@ -506,14 +557,16 @@
     rs_mid(6)
     rs_mid(4)
     first = (0, sj, seg, half_seg, pg1, gt1, hg)
-    weight_blocks(*first, 1)
+    weight_blocks(*first, 0)
     r_snd[2] = rs_end(5).astype(bf16)
     back_first = z_copy(5, r_snd.at[2], r_rcv.at[2], -1)
     go(back_first, z > 0)
+    weight_send(0, 0)
+    weight_blocks(*first, 1)
     weight_send(0, 1)
-    for d in range(2, tm):
-        weight_blocks(*first, d)
-        weight_send(0, d)
+    weight_relay(1)
+    weight_blocks(*first, 2)
+    weight_send(0, 2)
     own[6, 0] = hg[rows(w), :].astype(f32) + rs_end(6)
 
     @pl.when(z < tm - 1)
@@ -524,16 +577,22 @@
     gxs[rows(w), :] = own[6, 0].astype(bf16)
     g_gx = Gather(5, gxs, 0)
     g_gx.start()
-    weight_blocks(*second, 0)
+    weight_blocks(*second, 3)
     g_gx.forward()
-    weight_blocks(*first, 0)
+    weight_blocks(*first, 3)
     o_out2[...] = (hj[rows(w, 2 * seg), :].astype(f32) + rs_end(4)).astype(bf16)
     g_gx.finish()
     o_gx[...] = gxs[...]
+    weight_relay(0)
     weight_finish(1, o_cf2, o_cg2, o_mg2)
     weight_finish(0, o_cf1, o_cg1, o_mg1)
     for copy, cond in pending:
         when(cond, copy.wait_send)
+
+
+def hand_over(*refs):
+    for n in range(8):
+        refs[8 + n][...] = refs[n][...]
 
 
 def fused_body(*args):
@@ -546,7 +605,7 @@
     scale = 1.0 / math.sqrt(seg * tm)
     vm = pltpu.VMEM
     dma = pltpu.SemaphoreType.DMA
-    wide, others = 2 * cols, tm - 1
+    wide = 2 * cols
     scratch = [
         vm((2 * seg, chans), bf16),
         vm((3 * seg, chans), bf16),
@@ -571,29 +630,32 @@
         vm((7, 2, quarter, chans), f32),
         vm((3, quarter, chans), bf16),
         vm((3, quarter, chans), bf16),
-        vm((2, others, 3 * cblk, wide), bf16),
-        vm((2, others, 3 * cblk, wide), bf16),
+        vm((2, 3, 3 * cblk, wide), bf16),
+        vm((2, 4, 3 * cblk, wide), bf16),
         vm((2, 3 * cblk, wide), f32),
-        vm((2, others, cols, cblk), bf16),
-        vm((2, others, cols, cblk), bf16),
+        vm((2, 3 * cblk, wide), f32),
+        vm((2, 3, cols, cblk), bf16),
+        vm((2, 4, cols, cblk), bf16),
+        vm((2, cols, cblk), f32),
         vm((2, cols, cblk), f32),
         dma((4,)),
         dma((7, 2)), dma((7, 2)), dma((7,)), dma((7,)),
         dma((6, 3)), dma((6, 3)),
         dma((6,)), dma((6,)),
-        dma((2, others)), dma((2, others)), dma((2, others)), dma((2, others)),
+        dma((2, 3)), dma((2, 4)), dma((2, 3)), dma((2, 4)),
     ]
     conv = jax.ShapeDtypeStruct((3, cblk, cols), f32)
     mix = jax.ShapeDtypeStruct((cols, cblk), f32)
     in_vm = pl.BlockSpec(memory_space=pltpu.VMEM)
     in_any = pl.BlockSpec(memory_space=pl.ANY)
-    return pl.pallas_call(
+    shapes = (
+        jax.ShapeDtypeStruct((quarter, chans), bf16),
+        jax.ShapeDtypeStruct((seg, chans), bf16),
+        conv, conv, mix, conv, conv, mix,
+    )
+    results = pl.pallas_call(
         functools.partial(fused_kernel, tm, scale),
-        out_shape=(
-            jax.ShapeDtypeStruct((quarter, chans), bf16),
-            jax.ShapeDtypeStruct((seg, chans), bf16),
-            conv, conv, mix, conv, conv, mix,
-        ),
+        out_shape=shapes,
         in_specs=[in_vm, in_vm, in_any, in_any, in_vm, in_any, in_any, in_vm],
         out_specs=(in_vm,) * 8,
         scratch_shapes=scratch,
@@ -601,10 +663,16 @@
             collective_id=0, has_side_effects=True, vmem_limit_bytes=56 * 1024 * 1024
         ),
     )(*args)
+    return pl.pallas_call(
+        hand_over,
+        out_shape=shapes,
+        in_specs=[in_vm] * 8,
+        out_specs=(in_vm,) * 8,
+    )(*results)
 
 
 def fits(mesh):
-    return mesh.shape["wt"] == 4 and 3 <= mesh.shape["tm"] <= 4
+    return mesh.shape["wt"] == 4 and mesh.shape["tm"] == 4
 
 
 def solution(mesh):

time: 155 us -> 130 us (0.84)
  the two profiles are of different devices: /device:TPU:9 before, /device:TPU:0 now
where the time goes in v2:
time: 130 us; the launch traced here: 129 us
  Pallas kernels  129 us (99%)
    pallas_call x1, Pallas kernels, fused_body(): pl.pallas_call(functools.partial(fused_kernel, tm, scale), out_shape=shap...  126 us
    pallas_call x1, Pallas kernels, fused_body(): pl.pallas_call(hand_over, out_shape=shapes, in_specs=[in_vm] * 8, out_spe...  3.2 us

profile of v2, /device:TPU:0, one launch (start us, length us, event | category | flops | bytes accessed | tf_op | source)
XLA Modules:
  0.0 129.4 jit_solution(11772627452649644244)
XLA Ops:
  0.6 125.6 %shard_map.143 = (bf16[160,512]{1,0:T(8,128)(2,1)}, bf16[640,512]{1,0:T(8,128)(2,1)}, f32[3,128,256]{2,1,0:T(8,128)}, f32[3,128,256]{2,1,0:T(8,128)}, f32[256,12...) custom-call(bf16[640,512]{1,0:T(8,128)(2,1)} %sig.1, bf16[640,512]{1,0:T(8,128)(2,1)} %cot.1, ...), custom_call_target="tpu_custom_call" | custom-call | tf_op jit(solution)/shard_map/pallas_call | solution.py:656
  126.2 3.2 %shard_map.144 = (bf16[160,512]{1,0:T(8,128)(2,1)}, bf16[640,512]{1,0:T(8,128)(2,1)}, f32[3,128,256]{2,1,0:T(8,128)}, f32[3,128,256]{2,1,0:T(8,128)}, f32[256,12...) custom-call(bf16[160,512]{1,0:T(8,128)(2,1)} %get-tuple-element.16.refs_0_, ...), custom_call_target="tpu_custom_call" | custom-call | tf_op jit(solution)/shard_map/pallas_call | solution.py:666

commit v3 on v2

--- a/solution.py
+++ b/solution.py
@@ -552,17 +552,17 @@
         return dot_t(pg1[rows(q), :], w1[0]) + early * dot_t(pg1[rows(shifted_q), :], w1[1])
 
     rs_start(5, to_earlier)
+    first = (0, sj, seg, half_seg, pg1, gt1, hg)
+    weight_blocks(*first, 0)
+    weight_send(0, 0)
     rs_mid(5)
     rs_start(6, to_here)
     rs_mid(6)
     rs_mid(4)
-    first = (0, sj, seg, half_seg, pg1, gt1, hg)
-    weight_blocks(*first, 0)
+    weight_blocks(*first, 1)
     r_snd[2] = rs_end(5).astype(bf16)
     back_first = z_copy(5, r_snd.at[2], r_rcv.at[2], -1)
     go(back_first, z > 0)
-    weight_send(0, 0)
-    weight_blocks(*first, 1)
     weight_send(0, 1)
     weight_relay(1)
     weight_blocks(*first, 2)

time: 130 us -> 130 us (level)
  no operation moved by 1% of the time
where the time goes in v3:
time: 130 us; the launch traced here: 129 us
  Pallas kernels  129 us (99%)
    pallas_call x1, Pallas kernels, fused_body(): pl.pallas_call(functools.partial(fused_kernel, tm, scale), out_shape=shap...  126 us
    pallas_call x1, Pallas kernels, fused_body(): pl.pallas_call(hand_over, out_shape=shapes, in_specs=[in_vm] * 8, out_spe...  3.2 us

profile of v3, /device:TPU:0, one launch (start us, length us, event | category | flops | bytes accessed | tf_op | source)
XLA Modules:
  0.0 129.4 jit_solution(8490079133971579298)
XLA Ops:
  0.6 125.6 %shard_map.143 = (bf16[160,512]{1,0:T(8,128)(2,1)}, bf16[640,512]{1,0:T(8,128)(2,1)}, f32[3,128,256]{2,1,0:T(8,128)}, f32[3,128,256]{2,1,0:T(8,128)}, f32[256,12...) custom-call(bf16[640,512]{1,0:T(8,128)(2,1)} %sig.1, bf16[640,512]{1,0:T(8,128)(2,1)} %cot.1, ...), custom_call_target="tpu_custom_call" | custom-call | tf_op jit(solution)/shard_map/pallas_call | solution.py:656
  126.2 3.2 %shard_map.144 = (bf16[160,512]{1,0:T(8,128)(2,1)}, bf16[640,512]{1,0:T(8,128)(2,1)}, f32[3,128,256]{2,1,0:T(8,128)}, f32[3,128,256]{2,1,0:T(8,128)}, f32[256,12...) custom-call(bf16[160,512]{1,0:T(8,128)(2,1)} %get-tuple-element.16.refs_0_, ...), custom_call_target="tpu_custom_call" | custom-call | tf_op jit(solution)/shard_map/pallas_call | solution.py:666
